TPU v7x, 256 devices: a whole 4x4x8 slice. The times are simulated.
256 devices in a mesh: seq: 16 (over z, x_hi), head: 16 (over y, x_lo, core).
Axes of the slice: x: 4 (x_hi: 2, x_lo: 2; x = x_hi * 2 + x_lo), y: 4, z: 8, core: 2. Of those that a mesh axis runs over, the one named last changes fastest.
Arguments:
- q_latent: bfloat16 [2048, 1536], P('seq'), may hold values from -6 to 6
- kv_new: bfloat16 [2048, 576], P('seq'), may hold values from -6 to 6
- cache: bfloat16 [3072, 576], P('seq'), may hold values from -56 to 56
- latent_gain: float32 [512], replicated, may hold values from 0.1 to 1.9
- positions: int32 [2048], P('seq'), may hold values from 0 to 2047, as said below
- w_uq: bfloat16 [1536, 24576], P(None, 'head'), may hold values from -0.15625 to 0.15625
- w_uk: bfloat16 [128, 128, 512], P('head'), may hold values from -0.5 to 0.5
- w_uv: bfloat16 [128, 512, 128], P('head'), may hold values from -1 to 1
- w_out: bfloat16 [16384, 7168], P('head', 'seq'), may hold values from -0.1875 to 0.1875
Outputs:
- attended: bfloat16 [2048, 7168], P('seq', 'head')
Inputs may be any that keep to these rules, and one draw needn't show every extreme that they name: positions holds every number below 2048 once; each aligned block of 64 rows holds consecutive rising numbers starting at a multiple of 64.
All inputs are finite; a program needn't handle non-finite values.
Results may differ from a plain program's by a relative error of at most 0.025.
Values may be sent and summed in bfloat16 or wider, within the bound.
No kernel may reach another device: no remote copies, remote signals or barrier semaphores. Data moves between devices by JAX's collectives and lax.ppermute only.
A program may use at most 128 MiB of HBM per device.

v0:
```python
import math

import jax
import jax.numpy as jnp
from jax import lax
from jax.sharding import PartitionSpec as P

KV_RANK = 512
ROPE = 64
NOPE = 128
VDIM = 128


def angles(place, width):
    index = jnp.arange(width // 2, dtype=jnp.float32)
    inv_freq = jnp.exp(index * (-2.0 * math.log(10000.0) / width))
    return place[:, None] * inv_freq[None, :]


def rotate(vector, angle):
    half = vector.shape[-1] // 2
    first = vector[..., :half]
    second = vector[..., half:]
    cosine = jnp.cos(angle)
    sine = jnp.sin(angle)
    return jnp.concatenate(
        [first * cosine - second * sine, first * sine + second * cosine], axis=-1
    )


def per_device(q_latent, kv_new, cache, latent_gain, positions, w_uq, w_uk, w_uv, w_out):
    rows = q_latent.shape[0]
    heads = w_uk.shape[0]
    seq_count = lax.axis_size("seq")
    prefix_len = cache.shape[0] * seq_count
    query = jnp.dot(q_latent, w_uq, preferred_element_type=jnp.float32).astype(jnp.bfloat16)
    query = query.reshape(rows, heads, NOPE + ROPE)
    absorbed = jnp.einsum(
        "thn,hnc->thc", query[:, :, :NOPE], w_uk, preferred_element_type=jnp.float32
    ).astype(jnp.bfloat16)
    angle = angles((positions + prefix_len).astype(jnp.float32), ROPE)
    q_rot = rotate(query[:, :, NOPE:].astype(jnp.float32), angle[:, None, :]).astype(jnp.bfloat16)
    joined = jnp.concatenate([absorbed, q_rot], axis=-1)
    latent = kv_new[:, :KV_RANK].astype(jnp.float32)
    square = jnp.mean(latent * latent, axis=-1, keepdims=True) + 1e-06
    normed = latent / jnp.sqrt(square) * latent_gain[None, :]
    rotated = rotate(kv_new[:, KV_RANK:].astype(jnp.float32), angle)
    fresh = jnp.concatenate([normed, rotated], axis=-1).astype(jnp.bfloat16)
    scale = (NOPE + ROPE) ** (-0.5)

    def absorb_keys(carry, piece, allowed):
        top, total, accum = carry
        scores = (
            jnp.einsum("thc,kc->thk", joined, piece, preferred_element_type=jnp.float32) * scale
        )
        if allowed is not None:
            scores = jnp.where(allowed[:, None, :], scores, -1e30)
        new_top = jnp.maximum(top, jnp.max(scores, axis=-1))
        factor = jnp.exp(top - new_top)
        weights = jnp.exp(scores - new_top[:, :, None])
        total = total * factor + jnp.sum(weights, axis=-1)
        mixed = jnp.einsum(
            "thk,kc->thc",
            weights.astype(jnp.bfloat16),
            piece[:, :KV_RANK],
            preferred_element_type=jnp.float32,
        )
        accum = accum * factor[:, :, None] + mixed
        return (new_top, total, accum)

    start_state = (
        jnp.full((rows, heads), -1e30, jnp.float32),
        jnp.zeros((rows, heads), jnp.float32),
        jnp.zeros((rows, heads, KV_RANK), jnp.float32),
    )
    state = absorb_keys(start_state, lax.all_gather(cache, "seq", axis=0, tiled=True), None)
    piece = lax.all_gather(fresh, "seq", axis=0, tiled=True)
    key_place = lax.all_gather(positions, "seq", axis=0, tiled=True)
    allowed = key_place[None, :] <= positions[:, None]
    top, total, accum = absorb_keys(state, piece, allowed)
    latent_out = (accum / total[:, :, None]).astype(jnp.bfloat16)
    values = jnp.einsum(
        "thc,hcv->thv", latent_out, w_uv, preferred_element_type=jnp.float32
    ).astype(jnp.bfloat16)
    values = values.reshape(rows, heads * VDIM)
    partial_rows = jnp.dot(
        values, lax.all_gather(w_out, "seq", axis=1, tiled=True), preferred_element_type=jnp.float32
    )
    return lax.psum_scatter(
        partial_rows.astype(jnp.bfloat16), "head", scatter_dimension=1, tiled=True
    )


def solution(mesh):
    placed = (
        P("seq", None),
        P("seq", None),
        P("seq", None),
        P(),
        P("seq"),
        P(None, "head"),
        P("head", None, None),
        P("head", None, None),
        P("head", "seq"),
    )
    return jax.shard_map(
        per_device, mesh=mesh, in_specs=placed, out_specs=P("seq", "head"), check_vma=False
    )
```

profile of v0, /device:TPU:26, one launch (start us, length us, event | category | flops | bytes accessed | tf_op | source)
XLA Modules:
  0.0 475.1 jit_solution(10147356100259279107)
XLA Ops:
  6.5 0.8 slice_convert_fusion
  7.4 1.0 fusion.31
  8.3 0.7 add_convert_fusion.2
  9.0 1.1 fusion.33
  10.2 0.7 pad_maximum_fusion.3
  11.0 0.7 all-gather.5.cloned.1.call-update
  11.7 0.7 all-gather.9.cloned.1.call-update
  12.7 3.3 convolution_convert_fusion.1
  15.9 0.2 copy.25
  16.4 42.7 %all-gather = s32[16,1,128]{2,1,0:T(1,128)S(1)} all-gather(s32[1,1,128]{2,1,0:T(1,128)S(1)} %bitcast.39), channel_id=1, replica_groups=mesh['seq'=16,'head'=16] {'seq'}, dimensions={0}, use_global_device_ids=true | all-gather | bytes 8704 | tf_op jit(solution)/shard_map/all_gather | solution.py:78
  59.2 0.3 subtract_convert_fusion
  59.4 0.5 fusion.21
  59.9 0.2 broadcast_compare_fusion
  60.1 40.3 %all-gather.7.cloned.1.call-done = bf16[2048,576]{0,1:T(8,128)(2,1)} async-done(((bf16[128,576]{0,1:T(8,128)(2,1)}), bf16[2048,576]{0,1:T(8,128)(2,1)}) %all-gather.7.cloned.1.call-update) | async-done | bytes 2359312 | tf_op jit(solution)/shard_map/all_gather | solution.py:77
  100.4 8.0 %fusion.2 = (f32[128,8]{0,1:T(8,128)S(1)}, f32[128,8,2048]{2,0,1:T(8,128)}) fusion(pred[128,2048]{1,0:T(8,128)(4,1)S(1)} %broadcast_compare_fusion, bf16[2048,576]{0,1:T(8,128)(2,1)} %all-gather.7.cloned.1.call-done, bf16[128,8,32]{2,0,1:T(8,128)(2,1)S(1)} %get-tuple-element.8, bf16[128,8,32]{2,0,1:T(8,128)(2,1)S(1)} %get-tuple-element.7, ...), kind=kOutput, calls=%fused_computation.7 | convolution fusion | flops 2425748480 | bytes 12193792 | tf_op jit(solution)/shard_map/thc,kc->thk/dot_general | solution.py:54
  108.4 89.7 %all-gather.5.cloned.1.call-done = bf16[3072,576]{1,0:T(8,128)(2,1)} async-done(((bf16[192,576]{1,0:T(8,128)(2,1)}), bf16[3072,576]{1,0:T(8,128)(2,1)}) %all-gather.5.cloned.1.call-update) | async-done | bytes 3538960 | tf_op jit(solution)/shard_map/all_gather | solution.py:76
  198.1 7.4 %multiply_reduce_fusion = (f32[128,8]{0,1:T(8,128)S(1)}, f32[128,8,3072]{2,0,1:T(8,128)S(1)}) fusion(bf16[3072,576]{1,0:T(8,128)(2,1)} %all-gather.5.cloned.1.call-done, bf16[128,8,32]{2,0,1:T(8,128)(2,1)S(1)} %get-tuple-element.8, bf16[128,8,32]{2,0,1:T(8,128)(2,1)S(1)} %get-tuple-element.7, bf16[128,8,512]{2,0,1:T(8,128)(2,1)S(1)} %fusion.21), kind=kOutput, calls=%fused_computation.1 | convolution fusion | flops 3633708032 | bytes 17305600 | tf_op jit(solution)/shard_map/thc,kc->thk/dot_general | solution.py:54
  205.5 2.4 fusion.3
  208.0 2.2 fusion
  210.2 7.2 %fusion.5 = f32[128,8,512]{2,0,1:T(8,128)} fusion(f32[128,8,3072]{2,0,1:T(8,128)S(1)} %get-tuple-element.17, f32[128,8]{0,1:T(8,128)S(1)} %get-tuple-element.13, bf16[3072,576]{1,0:T(8,128)(2,1)} %all-gather.5.cloned.1.call-done), kind=kOutput, calls=%fused_computation.10 | convolution fusion | flops 3230662656 | bytes 17829888 | tf_op jit(solution)/shard_map/thk,kc->thc/dot_general | solution.py:62
  217.4 7.9 %fusion.25 = bf16[8,128,128]{1,2,0:T(8,128)(2,1)S(1)} fusion(bf16[8,512,128]{2,1,0:T(8,128)(2,1)S(1)} %copy-done.3, f32[128,8,512]{2,0,1:T(8,128)} %fusion.5, bf16[2048,576]{0,1:T(8,128)(2,1)} %all-gather.7.cloned.1.call-done, f32[128,8,2048]{2,0,1:T(8,128)} %get-tuple-element.19, f32[128,8]{0,1:T(8,128)S(1)} %get-tuple-element.12, ...), kind=kOutput, calls=%fused_computation.30 | convolution fusion | flops 2292842496 | bytes 14172160 | tf_op jit(solution)/shard_map/thc,hcv->thv/dot_general | solution.py:82
  225.3 173.5 %all-gather.9.cloned.1.call-done = bf16[1024,7168]{0,1:T(8,128)(2,1)} async-done(((bf16[1024,448]{0,1:T(8,128)(2,1)}), bf16[1024,7168]{0,1:T(8,128)(2,1)}) %all-gather.9.cloned.1.call-update) | async-done | bytes 14680080 | tf_op jit(solution)/shard_map/all_gather | solution.py:87
  398.9 10.4 %convolution_convert_fusion = bf16[128,7168]{0,1:T(8,128)(2,1)} fusion(bf16[1024,7168]{0,1:T(8,128)(2,1)} %all-gather.9.cloned.1.call-done, bf16[128,1024]{0,1:T(8,128)(2,1)S(1)} %bitcast.40), kind=kOutput, calls=%fused_computation.4 | convolution fusion | flops 1879965696 | bytes 16777216 | tf_op jit(solution)/shard_map/dot_general | solution.py:86
  409.3 59.2 %reduce-scatter.2.cloned.1.call-done = bf16[128,448]{0,1:T(8,128)(2,1)} async-done(((bf16[128,7168]{0,1:T(8,128)(2,1)}), bf16[128,448]{0,1:T(8,128)(2,1)}) %reduce-scatter.2.cloned.1.call-update) | async-done | bytes 114704 | tf_op jit(solution)/shard_map/reduce_scatter | solution.py:89
  (24 shorter events, 0.8 us)
Async XLA Ops:
  6.5 52.9 %copy-start = (bf16[8,128,512]{2,1,0:T(8,128)(2,1)S(1)}, bf16[8,128,512]{2,1,0:T(8,128)(2,1)}, u32[]{:S(2)}) copy-start(bf16[8,128,512]{2,1,0:T(8,128)(2,1)} %param.15) | copy-start | bytes 3145732
  6.5 93.9 %all-gather.7.cloned.1.call-start = ((), (), s32[]{:S(2)}) async-start(), calls=%async_computation.2 | async-start | bytes 2506752 | tf_op jit(solution)/shard_map/all_gather | solution.py:77
  10.9 187.2 %all-gather.5.cloned.1.call-start = ((), (), s32[]{:S(2)}) async-start(), calls=%async_computation.1 | async-start | bytes 4177920 | tf_op jit(solution)/shard_map/all_gather | solution.py:76
  11.7 387.2 %all-gather.9.cloned.1.call-start = ((), (), s32[]{:S(2)}) async-start(), calls=%async_computation.3 | async-start | bytes 15597568 | tf_op jit(solution)/shard_map/all_gather | solution.py:87
  12.4 456.1 %reduce-scatter.2.cloned.1.call-start = ((), (), s32[]{:S(2)}) async-start(), calls=%async_computation.4 | async-start | bytes 1949696 | tf_op jit(solution)/shard_map/reduce_scatter | solution.py:89
  12.5 4.0 copy-start.2
  198.1 7.4 %copy-start.1 = (f32[128,8,2048]{2,0,1:T(8,128)S(1)}, f32[128,8,2048]{2,0,1:T(8,128)}, u32[]{:S(2)}) copy-start(f32[128,8,2048]{2,0,1:T(8,128)} %get-tuple-element.19) | copy-start | bytes 25165828
  210.2 7.2 %copy-start.3 = (bf16[8,512,128]{2,1,0:T(8,128)(2,1)S(1)}, bf16[8,512,128]{2,1,0:T(8,128)(2,1)}, u32[]{:S(2)}) copy-start(bf16[8,512,128]{2,1,0:T(8,128)(2,1)} %param.16) | copy-start | bytes 3145732
Sparse Core Ops, SparseCore 0:
  11.1 89.3 all-gather.6
  103.0 95.0 all-gather.4
  200.7 198.1 all-gather.8
  409.4 59.0 reduce-scatter.1
where the time goes:
time: 480 us; the launch traced here: 475 us
  waiting for transfers between devices  364 us (76%)
  matrix products  44.7 us (9%)
  blocking collectives  42.7 us (9%)
  between operations  13.3 us (3%)
  other arithmetic  9.49 us (2%)
    all_gather x1, waiting for transfers between devices, per_device(): lax.all_gather(w_out, 'seq', axis=1, tiled=True)  174 us
    all_gather x1, waiting for transfers between devices, per_device(): lax.all_gather(cache, 'seq', axis=0, tiled=True)  89.7 us
    reduce_scatter x1, waiting for transfers between devices, per_device(): lax.psum_scatter(partial_rows.astype(jnp.bfloat16), 'head', scatter_dimen...  59.2 us
    all_gather x1, blocking collectives, per_device(): key_place = lax.all_gather(positions, 'seq', axis=0, tiled=True)  42.7 us
    all_gather x1, waiting for transfers between devices, per_device(): piece = lax.all_gather(fresh, 'seq', axis=0, tiled=True)  40.3 us
    dot_general x2, matrix products, absorb_keys(): jnp.einsum('thc,kc->thk', joined, piece, preferred_element_type=jnp.float32)  15.4 us
    dot_general x1, matrix products, per_device(): jnp.dot(values, lax.all_gather(w_out, 'seq', axis=1, tiled=True), preferr...  10.4 us
  transfers between devices with their start and end apart: 4, of which 4 were waited for; matrix products, arithmetic and copies ran while one was open for 8% of the time, Pallas kernels for 0%

commit v1 on v0

v1 whole, which is shorter than its diff:
```python
import functools
import math

import jax
import jax.numpy as jnp
from jax import lax
from jax.experimental import pallas as pl
from jax.experimental.pallas import tpu as pltpu
from jax.sharding import PartitionSpec as P

KV_RANK = 512
ROPE = 64
NOPE = 128
VDIM = 128
RUN = 64
PREFIX = 3072
WIDE = 640
AXES = ("seq", "head")
BIG = -1e30
F32 = jnp.float32
BF16 = jnp.bfloat16


def place_of(i):
    s, h = divmod(i, 16)
    return s // 2, s % 2, h // 4, (h // 2) % 2, h % 2


def index_of(z, xh, y, xl, c):
    return (z * 2 + xh) * 16 + y * 4 + xl * 2 + c


def pairs(to):
    return [(i, index_of(*to(*place_of(i)))) for i in range(256)]


def shift_z(d):
    return pairs(lambda z, xh, y, xl, c: ((z + d) % 8, xh, y, xl, c))


def shift_y(d):
    return pairs(lambda z, xh, y, xl, c: (z, xh, (y + d) % 4, xl, c))


SWAP_CORE = pairs(lambda z, xh, y, xl, c: (z, xh, y, xl, 1 - c))
SWAP_XH = pairs(lambda z, xh, y, xl, c: (z, 1 - xh, y, xl, c))
SWAP_MIRROR = pairs(lambda z, xh, y, xl, c: (z, 1 - xh, y, 1 - xl, c))

ORDER = (0, 1, -1, 2, -2, 3, -3, 4)


def final_pairs(same):
    def to(z, xh, y, xl, c):
        piece = 2 * y + (xl if same else 1 - xl)
        return (z + ORDER[piece]) % 8, xh, z >> 1, z & 1, c

    return pairs(to)


def permute(x, perm):
    return lax.ppermute(x, AXES, perm)


def angles(place, width):
    index = jnp.arange(width // 2, dtype=F32)
    inv_freq = jnp.exp(index * (-2.0 * math.log(10000.0) / width))
    return place[:, None] * inv_freq[None, :]


def query_kernel(lat_ref, wq_ref, wk_ref, cos_ref, sin_ref, mask_ref, out_ref):
    scale = (NOPE + ROPE) ** (-0.5) * math.log2(math.e)
    query = jnp.dot(lat_ref[...], wq_ref[...], preferred_element_type=F32).astype(BF16)
    for i in range(2):
        part = query[:, i * 192 : (i + 1) * 192]
        absorbed = jnp.dot(part[:, :NOPE], wk_ref[i], preferred_element_type=F32)
        out_ref[i, :, :KV_RANK] = (absorbed * scale).astype(BF16)
        rope = part[:, NOPE:].astype(F32)
        swapped = jnp.concatenate([rope[:, ROPE // 2 :], rope[:, : ROPE // 2]], axis=1)
        rotated = rope * cos_ref[...] + swapped * sin_ref[...]
        out_ref[i, :, KV_RANK:] = jnp.concatenate(
            [(rotated * scale).astype(BF16), mask_ref[...]], axis=1
        )


def queries(lat, w_uq, w_uk, cosine, sine, mask):
    rows = lat.shape[0]
    heads = w_uk.shape[0]
    whole = lambda i: (0, 0)
    return pl.pallas_call(
        query_kernel,
        grid=(heads // 2,),
        in_specs=[
            pl.BlockSpec(lat.shape, whole),
            pl.BlockSpec((w_uq.shape[0], 384), lambda i: (0, i)),
            pl.BlockSpec((2, NOPE, KV_RANK), lambda i: (i, 0, 0)),
            pl.BlockSpec(cosine.shape, whole),
            pl.BlockSpec(sine.shape, whole),
            pl.BlockSpec(mask.shape, whole),
        ],
        out_specs=pl.BlockSpec((2, rows, WIDE), lambda i: (i, 0, 0)),
        out_shape=jax.ShapeDtypeStruct((heads, rows, WIDE), BF16),
        compiler_params=pltpu.CompilerParams(vmem_limit_bytes=32 * 2**20),
        cost_estimate=pl.CostEstimate(
            flops=2 * rows * heads * (1536 * 192 + 128 * 512),
            bytes_accessed=10 * 2**20,
            transcendentals=0,
        ),
    )(lat, w_uq, w_uk, cosine, sine, mask)


def attend_kernel(q_ref, ka_ref, kb_ref, bias_ref, wv_ref, out_ref, top_ref, total_ref, s_ref):
    nt = (((1,), (1,)), ((), ()))
    group, rows = q_ref.shape[0], q_ref.shape[1]
    half = ka_ref.shape[0]
    for i in range(group):
        q = q_ref[i]
        tops = []
        for part, keys in enumerate((ka_ref, kb_ref)):
            for j in range(half // 256):
                scores = lax.dot_general(
                    q, keys[j * 256 : (j + 1) * 256, :], nt, preferred_element_type=F32
                )
                if j == 0:
                    scores = scores + bias_ref[part]
                at = part * half + j * 256
                s_ref[:, at : at + 256] = scores
                tops.append(jnp.maximum(scores[:, :128], scores[:, 128:]))
        top = functools.reduce(jnp.maximum, tops)
        top = jnp.max(top, axis=1, keepdims=True)
        total = jnp.zeros((rows, 128), F32)
        accum = jnp.zeros((rows, KV_RANK), F32)
        for part, keys in enumerate((ka_ref, kb_ref)):
            for j in range(half // 256):
                at = part * half + j * 256
                weights = jnp.exp2(s_ref[:, at : at + 256] - top)
                total = total + (weights[:, :128] + weights[:, 128:])
                accum = accum + jnp.dot(
                    weights.astype(BF16),
                    keys[j * 256 : (j + 1) * 256, :KV_RANK],
                    preferred_element_type=F32,
                )
        total = jnp.sum(total, axis=1, keepdims=True)
        latent = (accum / total).astype(BF16)
        out_ref[:, i * VDIM : (i + 1) * VDIM] = jnp.dot(
            latent, wv_ref[i], preferred_element_type=F32
        ).astype(BF16)
        top_ref[i] = jnp.broadcast_to(top, (rows, 128))
        total_ref[i] = jnp.broadcast_to(total, (rows, 128))


def attend(q, ka, kb, bias, w_uv):
    heads, rows, _ = q.shape
    half = ka.shape[0]
    group = 2
    stat = jax.ShapeDtypeStruct((heads, rows, 128), F32)
    stat_spec = pl.BlockSpec((group, rows, 128), lambda i: (i, 0, 0))
    return pl.pallas_call(
        attend_kernel,
        grid=(heads // group,),
        in_specs=[
            pl.BlockSpec((group, rows, WIDE), lambda i: (i, 0, 0)),
            pl.BlockSpec(ka.shape, lambda i: (0, 0)),
            pl.BlockSpec(kb.shape, lambda i: (0, 0)),
            pl.BlockSpec(bias.shape, lambda i: (0, 0, 0)),
            pl.BlockSpec((group, KV_RANK, VDIM), lambda i: (i, 0, 0)),
        ],
        out_specs=[
            pl.BlockSpec((rows, group * VDIM), lambda i: (0, i)),
            stat_spec,
            stat_spec,
        ],
        out_shape=[jax.ShapeDtypeStruct((rows, heads * VDIM), BF16), stat, stat],
        scratch_shapes=[pltpu.VMEM((rows, 2 * half), F32)],
        compiler_params=pltpu.CompilerParams(vmem_limit_bytes=48 * 2**20),
        cost_estimate=pl.CostEstimate(
            flops=2 * rows * heads * 2 * half * (WIDE + KV_RANK),
            bytes_accessed=10 * 2**20,
            transcendentals=rows * heads * 2 * half,
        ),
    )(q, ka, kb, bias, w_uv)


def ring(own):
    rows = own.shape[0]
    up, down = own, own
    got = [own]
    for _ in range(3):
        up = permute(up, shift_z(1))
        down = permute(down, shift_z(-1))
        got += [down, up]
    far_up = permute(up[: rows // 2], shift_z(1))
    far_down = permute(down[rows // 2 :], shift_z(-1))
    return got + [far_up, far_down]


def per_device(q_latent, kv_new, cache, latent_gain, positions, w_uq, w_uk, w_uv, w_out):
    rows = q_latent.shape[0]
    heads = w_uk.shape[0]
    head_index = lax.axis_index("head")
    seq_index = lax.axis_index("seq")
    core = head_index % 2
    x_hi = seq_index % 2

    run = positions // RUN
    lane = jnp.arange(128)[None, :]
    marks = jnp.where(
        lane == 0, run[:, None], jnp.where(lane == 1, (positions % RUN)[:, None], 0)
    ).astype(BF16)
    sent = jnp.concatenate([q_latent, marks], axis=1)
    other = permute(sent, SWAP_MIRROR)
    w_other = permute(w_out, SWAP_XH)

    place = (positions + PREFIX).astype(F32)
    angle = angles(place, ROPE)
    cos_own, sin_own = jnp.cos(angle), jnp.sin(angle)
    latent = kv_new[:, :KV_RANK].astype(F32)
    square = jnp.mean(latent * latent, axis=-1, keepdims=True) + 1e-06
    normed = latent / jnp.sqrt(square) * latent_gain[None, :]
    rope = kv_new[:, KV_RANK:].astype(F32)
    first, second = rope[:, : ROPE // 2], rope[:, ROPE // 2 :]
    one_hot = (run[:, None] == jnp.arange(WIDE - KV_RANK - ROPE)[None, :]).astype(F32)
    fresh = jnp.concatenate(
        [
            normed,
            first * cos_own - second * sin_own,
            first * sin_own + second * cos_own,
            one_hot,
        ],
        axis=1,
    ).astype(BF16)
    old = jnp.pad(cache, ((0, 0), (0, WIDE - KV_RANK - ROPE)))
    old_rows = old.shape[0] // 2
    own = jnp.concatenate(
        [
            lax.dynamic_slice_in_dim(old, core * old_rows, old_rows, 0),
            lax.dynamic_slice_in_dim(fresh, core * RUN, RUN, 0),
        ],
        axis=0,
    )
    keys = jnp.concatenate(ring(own), axis=0)
    keys_other = permute(keys, SWAP_CORE)

    other_marks = other[:, 1536:1538].astype(jnp.int32)
    other_run = other_marks[:, 0]
    other_positions = other_run * RUN + other_marks[:, 1]
    other_angle = angles((other_positions + PREFIX).astype(F32), ROPE)
    cos = jnp.concatenate([cos_own, jnp.cos(other_angle)], axis=0)
    sin = jnp.concatenate([sin_own, jnp.sin(other_angle)], axis=0)
    both_run = jnp.concatenate([run, other_run], axis=0)
    mask = jnp.where(jnp.arange(WIDE - KV_RANK - ROPE)[None, :] > both_run[:, None], BIG, 0.0)
    lat = jnp.concatenate([q_latent, other[:, :1536]], axis=0)
    q = queries(
        lat,
        w_uq,
        w_uk,
        jnp.concatenate([cos, cos], axis=1),
        jnp.concatenate([-sin, sin], axis=1),
        mask.astype(BF16),
    )

    token = jnp.arange(2 * rows)[None, :, None]
    slot = jnp.arange(256)[None, None, :]
    of_core = jnp.stack([core, 1 - core])[:, None, None]
    hidden = (
        (token < rows)
        & (token // RUN == of_core)
        & (slot >= old_rows)
        & (slot < old_rows + RUN)
        & (slot - old_rows > token % RUN)
    )
    bias = jnp.where(hidden, BIG, 0.0).astype(F32)
    part, top, total = attend(q, keys, keys_other, bias, w_uv)

    lse = (top + jnp.log2(total))[:, :, 0].T
    lse_high = lse.astype(BF16)
    rest = lse - lse_high.astype(F32)
    lse_mid = rest.astype(BF16)
    lse_low = (rest - lse_mid.astype(F32)).astype(BF16)
    packed = jnp.concatenate(
        [
            part[rows:],
            lse_high[rows:],
            lse_mid[rows:],
            lse_low[rows:],
            jnp.zeros((rows, 128 - 3 * heads), BF16),
        ],
        axis=1,
    )
    came = permute(packed, SWAP_XH)
    wide = heads * VDIM
    came_lse = sum(
        came[:, wide + i * heads : wide + (i + 1) * heads].astype(F32) for i in range(3)
    )
    own_lse = lse[:rows]
    best = jnp.maximum(own_lse, came_lse)
    own_weight = jnp.exp2(own_lse - best)
    came_weight = jnp.exp2(came_lse - best)
    both = own_weight + came_weight
    spread = lambda w: jnp.repeat(w / both, VDIM, axis=1)
    values = (
        part[:rows].astype(F32) * spread(own_weight)
        + came[:, :wide].astype(F32) * spread(came_weight)
    ).astype(BF16)

    same = x_hi == core
    w_keep = jnp.where(same, w_out, w_other)
    w_send = jnp.where(same, w_other, w_out)
    values = jnp.concatenate(ring(values), axis=0)
    send = jnp.dot(values, w_send, preferred_element_type=F32).astype(BF16)
    came = permute(send, SWAP_CORE)
    keep = jnp.dot(values, w_keep, preferred_element_type=F32)
    summed = (keep + came.astype(F32)).astype(BF16)

    y = head_index // 4
    x_lo = (head_index // 2) % 2
    take = lambda at: lax.dynamic_slice_in_dim(summed, at * 2 * rows, 2 * rows, 0)
    parts = [permute(take((y + d) % 4), shift_y(d)) for d in (1, 3, 2)]
    mine = take(y).astype(F32) + sum(p.astype(F32) for p in parts)
    mine = mine.astype(BF16)
    straight = permute(lax.dynamic_slice_in_dim(mine, x_lo * rows, rows, 0), final_pairs(True))
    crossed = permute(
        lax.dynamic_slice_in_dim(mine, (1 - x_lo) * rows, rows, 0), final_pairs(False)
    )
    return (straight.astype(F32) + crossed.astype(F32)).astype(BF16)


def solution(mesh):
    placed = (
        P("seq", None),
        P("seq", None),
        P("seq", None),
        P(),
        P("seq"),
        P(None, "head"),
        P("head", None, None),
        P("head", None, None),
        P("head", "seq"),
    )
    return jax.shard_map(
        per_device, mesh=mesh, in_specs=placed, out_specs=P("seq", "head"), check_vma=False
    )
```

time: 480 us -> 170 us (0.35)
  the two profiles are of different devices: /device:TPU:26 before, /device:TPU:14 now
where the time goes in v1:
time: 170 us
  waiting for transfers between devices  80.3 us (47%)
  starting transfers between devices  46.7 us (27%)
  Pallas kernels  24.4 us (14%)
  local copies, waits for them, and re-layouts  7.35 us (4%)
  other arithmetic  5.24 us (3%)
  matrix products  4.94 us (3%)
    ppermute x26, waiting for transfers between devices, permute(): return lax.ppermute(x, AXES, perm)  80.3 us
    ppermute x26, starting transfers between devices, permute(): return lax.ppermute(x, AXES, perm)  46.7 us
    pallas_call x1, Pallas kernels, attend(): pl.pallas_call(attend_kernel, grid=(heads // group,), in_specs=[pl.BlockS...  20.4 us
    pallas_call x1, Pallas kernels, queries(): pl.pallas_call(query_kernel, grid=(heads // 2,), in_specs=[pl.BlockSpec(l...  4.01 us
  transfers between devices with their start and end apart: 26, of which 17 were waited for; matrix products, arithmetic and copies ran while one was open for 2% of the time, Pallas kernels for 2%

profile of v1, /device:TPU:14, one launch (start us, length us, event | category | flops | bytes accessed | tf_op | source)
XLA Modules:
  0.0 169.7 jit_solution(9484193992561032610)
XLA Ops:
  4.9 9.9 %collective-permute-done = bf16[128,1664]{1,0:T(8,128)(2,1)S(1)} collective-permute-done((bf16[128,1664]{1,0:T(8,128)(2,1)S(1)}, bf16[128,1664]{1,0:T(8,128)(2,1)S(1)}, u32[]{:S(2)}, u32[]{:S(2)}) %collective-permute-start) | collective-permute-done | bytes 426016 | tf_op jit(solution)/shard_map/ppermute | solution.py:61
  15.6 5.9 %collective-permute-start.1 = (bf16[160,640]{1,0:T(8,128)(2,1)S(1)}, bf16[160,640]{1,0:T(8,128)(2,1)S(1)}, u32[]{:S(2)}, u32[]{:S(2)}) collective-permute-start(bf16[160,640]{1,0:T(8,128)(2,1)S(1)} %pad_maximum_fusion.2), channel_id=1, source_target_pairs={{0,224},{1,225},{2,226},{3,227},{4,228},{5,229},{6,230},{7,231},{8... | collective-permute-start | bytes 614408 | tf_op jit(solution)/shard_map/ppermute | solution.py:61
  21.7 3.3 %collective-permute-done.1 = bf16[160,640]{1,0:T(8,128)(2,1)S(1)} collective-permute-done((bf16[160,640]{1,0:T(8,128)(2,1)S(1)}, bf16[160,640]{1,0:T(8,128)(2,1)S(1)}, u32[]{:S(2)}, u32[]{:S(2)}) %collective-permute-start.1) | collective-permute-done | bytes 204832 | tf_op jit(solution)/shard_map/ppermute | solution.py:61
  25.0 3.7 %collective-permute-start.3 = (bf16[160,640]{1,0:T(8,128)(2,1)S(1)}, bf16[160,640]{1,0:T(8,128)(2,1)S(1)}, u32[]{:S(2)}, u32[]{:S(2)}) collective-permute-start(bf16[160,640]{1,0:T(8,128)(2,1)S(1)} %collective-permute-done.1), channel_id=1, source_target_pairs={{0,224},{1,225},{2,226},{3,227},{4,228},{5,229},{6,230},{7,231},{8... | collective-permute-start | bytes 614408 | tf_op jit(solution)/shard_map/ppermute | solution.py:61
  28.8 3.2 %collective-permute-done.3 = bf16[160,640]{1,0:T(8,128)(2,1)S(1)} collective-permute-done((bf16[160,640]{1,0:T(8,128)(2,1)S(1)}, bf16[160,640]{1,0:T(8,128)(2,1)S(1)}, u32[]{:S(2)}, u32[]{:S(2)}) %collective-permute-start.3) | collective-permute-done | bytes 204832 | tf_op jit(solution)/shard_map/ppermute | solution.py:61
  32.0 3.7 %collective-permute-start.5 = (bf16[160,640]{1,0:T(8,128)(2,1)S(1)}, bf16[160,640]{1,0:T(8,128)(2,1)S(1)}, u32[]{:S(2)}, u32[]{:S(2)}) collective-permute-start(bf16[160,640]{1,0:T(8,128)(2,1)S(1)} %collective-permute-done.3), channel_id=1, source_target_pairs={{0,224},{1,225},{2,226},{3,227},{4,228},{5,229},{6,230},{7,231},{8... | collective-permute-start | bytes 614408 | tf_op jit(solution)/shard_map/ppermute | solution.py:61
  35.8 7.5 %collective-permute-done.6 = bf16[160,640]{1,0:T(8,128)(2,1)S(1)} collective-permute-done((bf16[160,640]{1,0:T(8,128)(2,1)S(1)}, bf16[160,640]{1,0:T(8,128)(2,1)S(1)}, u32[]{:S(2)}, u32[]{:S(2)}) %collective-permute-start.6) | collective-permute-done | bytes 204832 | tf_op jit(solution)/shard_map/ppermute | solution.py:61
  43.3 3.3 %collective-permute-start.8 = (bf16[80,640]{1,0:T(8,128)(2,1)S(1)}, bf16[80,640]{1,0:T(8,128)(2,1)S(1)}, u32[]{:S(2)}, u32[]{:S(2)}) collective-permute-start(bf16[80,640]{1,0:T(8,128)(2,1)S(1)} %slice.99), channel_id=1, source_target_pairs={{0,224},{1,225},{2,226},{3,227},{4,228},{5,229},{6,230},{7,231},{8... | collective-permute-start | bytes 307208 | tf_op jit(solution)/shard_map/ppermute | solution.py:61
  50.4 4.0 %shard_map.91.q_ref = bf16[8,256,640]{2,1,0:T(8,128)(2,1)S(1)} custom-call(bf16[256,1536]{1,0:T(8,128)(2,1)S(1)} %pad_maximum_fusion.lat_ref, bf16[1536,1536]{1,0:T(8,128)(2,1)S(1)} %copy-done, bf16[8,128,512]{2,1,0:T(8,128)(2,1)S(1)} %copy-done.2, f32[256,64]{1,0:T(8,128)S(1)} %maximum_maximum_fusion.cos_ref, f32[256,64]{1,0:T(8,128)S(1)} %maximum_maximum_fusion.1.sin_ref, ...), custom_call_target="tpu_custom_call" | custom-call | flops 1476395008 | bytes 10485760 | tf_op jit(solution)/shard_map/pallas_call | solution.py:89
  57.0 20.4 %shard_map.92 = (bf16[256,1024]{1,0:T(8,128)(2,1)S(1)}, f32[8,256,128]{2,1,0:T(8,128)S(1)}, f32[8,256,128]{2,1,0:T(8,128)S(1)}) custom-call(bf16[8,256,640]{2,1,0:T(8,128)(2,1)} %copy-done.1, bf16[1280,640]{1,0:T(8,128)(2,1)S(1)} %constant_dynamic-update-slice_fusion.ka_ref, bf16[1280,640]{1,0:T(8,128)(2,1)} %copy-done.7, ...), custom_call_target="tpu_custom_call" | custom-call | flops 12079595520 | bytes 10485760 | tf_op jit(solution)/shard_map/pallas_call | solution.py:157
  79.8 10.7 %collective-permute-done.10 = bf16[128,1152]{1,0:T(8,128)(2,1)S(1)} collective-permute-done((bf16[128,1152]{1,0:T(8,128)(2,1)S(1)}, bf16[128,1152]{1,0:T(8,128)(2,1)S(1)}, u32[]{:S(2)}, u32[]{:S(2)}) %collective-permute-start.10) | collective-permute-done | bytes 294944 | tf_op jit(solution)/shard_map/ppermute | solution.py:61
  91.3 3.4 %collective-permute-start.11 = (bf16[128,1024]{1,0:T(8,128)(2,1)S(1)}, bf16[128,1024]{1,0:T(8,128)(2,1)S(1)}, u32[]{:S(2)}, u32[]{:S(2)}) collective-permute-start(bf16[128,1024]{1,0:T(8,128)(2,1)S(1)} %get-tuple-element.12), channel_id=1, source_target_pairs={{0,224},{1,225},{2,226},{3,227},{4,228},{5,229},{6,230},{7,231},{8... | collective-permute-start | bytes 786440 | tf_op jit(solution)/shard_map/ppermute | solution.py:61
  94.7 5.4 %collective-permute-done.11 = bf16[128,1024]{1,0:T(8,128)(2,1)S(1)} collective-permute-done((bf16[128,1024]{1,0:T(8,128)(2,1)S(1)}, bf16[128,1024]{1,0:T(8,128)(2,1)S(1)}, u32[]{:S(2)}, u32[]{:S(2)}) %collective-permute-start.11) | collective-permute-done | bytes 262176 | tf_op jit(solution)/shard_map/ppermute | solution.py:61
  100.1 3.7 %collective-permute-start.13 = (bf16[128,1024]{1,0:T(8,128)(2,1)S(1)}, bf16[128,1024]{1,0:T(8,128)(2,1)S(1)}, u32[]{:S(2)}, u32[]{:S(2)}) collective-permute-start(bf16[128,1024]{1,0:T(8,128)(2,1)S(1)} %collective-permute-done.11), channel_id=1, source_target_pairs={{0,224},{1,225},{2,226},{3,227},{4,228},{5,229},{6,230},{7,231},{8... | collective-permute-start | bytes 786440 | tf_op jit(solution)/shard_map/ppermute | solution.py:61
  104.2 4.1 %collective-permute-done.13 = bf16[128,1024]{1,0:T(8,128)(2,1)S(1)} collective-permute-done((bf16[128,1024]{1,0:T(8,128)(2,1)S(1)}, bf16[128,1024]{1,0:T(8,128)(2,1)S(1)}, u32[]{:S(2)}, u32[]{:S(2)}) %collective-permute-start.13) | collective-permute-done | bytes 262176 | tf_op jit(solution)/shard_map/ppermute | solution.py:61
  108.4 3.7 %collective-permute-start.15 = (bf16[128,1024]{1,0:T(8,128)(2,1)S(1)}, bf16[128,1024]{1,0:T(8,128)(2,1)S(1)}, u32[]{:S(2)}, u32[]{:S(2)}) collective-permute-start(bf16[128,1024]{1,0:T(8,128)(2,1)S(1)} %collective-permute-done.13), channel_id=1, source_target_pairs={{0,224},{1,225},{2,226},{3,227},{4,228},{5,229},{6,230},{7,231},{8... | collective-permute-start | bytes 786440 | tf_op jit(solution)/shard_map/ppermute | solution.py:61
  112.1 7.5 %collective-permute-done.16 = bf16[128,1024]{1,0:T(8,128)(2,1)S(1)} collective-permute-done((bf16[128,1024]{1,0:T(8,128)(2,1)S(1)}, bf16[128,1024]{1,0:T(8,128)(2,1)S(1)}, u32[]{:S(2)}, u32[]{:S(2)}) %collective-permute-start.16) | collective-permute-done | bytes 262176 | tf_op jit(solution)/shard_map/ppermute | solution.py:61
  119.8 3.3 %collective-permute-start.18 = (bf16[64,1024]{1,0:T(8,128)(2,1)S(1)}, bf16[64,1024]{1,0:T(8,128)(2,1)S(1)}, u32[]{:S(2)}, u32[]{:S(2)}) collective-permute-start(bf16[64,1024]{1,0:T(8,128)(2,1)S(1)} %slice.112), channel_id=1, source_target_pairs={{0,224},{1,225},{2,226},{3,227},{4,228},{5,229},{6,230},{7,231},{8... | collective-permute-start | bytes 393224 | tf_op jit(solution)/shard_map/ppermute | solution.py:61
  123.1 2.8 %collective-permute-done.17 = bf16[64,1024]{1,0:T(8,128)(2,1)S(1)} collective-permute-done((bf16[64,1024]{1,0:T(8,128)(2,1)S(1)}, bf16[64,1024]{1,0:T(8,128)(2,1)S(1)}, u32[]{:S(2)}, u32[]{:S(2)}) %collective-permute-start.17) | collective-permute-done | bytes 131104 | tf_op jit(solution)/shard_map/ppermute | solution.py:61
  138.6 4.1 %collective-permute-done.21 = bf16[256,448]{0,1:T(8,128)(2,1)S(1)} collective-permute-done((bf16[256,448]{0,1:T(8,128)(2,1)S(1)}, bf16[256,448]{0,1:T(8,128)(2,1)S(1)}, u32[]{:S(2)}, u32[]{:S(2)}) %collective-permute-start.21) | collective-permute-done | bytes 229408 | tf_op jit(solution)/shard_map/ppermute | solution.py:61
  143.6 5.2 %collective-permute-done.23 = bf16[256,448]{0,1:T(8,128)(2,1)S(1)} collective-permute-done((bf16[256,448]{0,1:T(8,128)(2,1)S(1)}, bf16[256,448]{0,1:T(8,128)(2,1)S(1)}, u32[]{:S(2)}, u32[]{:S(2)}) %collective-permute-start.23) | collective-permute-done | bytes 229408 | tf_op jit(solution)/shard_map/ppermute | solution.py:61
  150.9 8.0 %collective-permute-start.25 = (bf16[128,448]{0,1:T(8,128)(2,1)S(1)}, bf16[128,448]{0,1:T(8,128)(2,1)S(1)}, u32[]{:S(2)}, u32[]{:S(2)}) collective-permute-start(bf16[128,448]{0,1:T(8,128)(2,1)S(1)} %get-tuple-element.23), channel_id=1, source_target_pairs={{0,32},{1,33},{2,0},{3,1},{4,64},{5,65},{6,224},{7,225},{8,96},{9,... | collective-permute-start | bytes 344072 | tf_op jit(solution)/shard_map/ppermute | solution.py:61
  158.9 2.6 %collective-permute-done.24 = bf16[128,448]{0,1:T(8,128)(2,1)S(1)} collective-permute-done((bf16[128,448]{0,1:T(8,128)(2,1)S(1)}, bf16[128,448]{0,1:T(8,128)(2,1)S(1)}, u32[]{:S(2)}, u32[]{:S(2)}) %collective-permute-start.24) | collective-permute-done | bytes 114720 | tf_op jit(solution)/shard_map/ppermute | solution.py:61
  161.5 7.5 %collective-permute-done.25 = bf16[128,448]{0,1:T(8,128)(2,1)S(1)} collective-permute-done((bf16[128,448]{0,1:T(8,128)(2,1)S(1)}, bf16[128,448]{0,1:T(8,128)(2,1)S(1)}, u32[]{:S(2)}, u32[]{:S(2)}) %collective-permute-start.25) | collective-permute-done | bytes 114720 | tf_op jit(solution)/shard_map/ppermute | solution.py:61
  (122 shorter events, 32.0 us)
Async XLA Ops:
  1.9 12.9 %collective-permute-start = (bf16[128,1664]{1,0:T(8,128)(2,1)S(1)}, bf16[128,1664]{1,0:T(8,128)(2,1)S(1)}, u32[]{:S(2)}, u32[]{:S(2)}) collective-permute-start(bf16[128,1664]{1,0:T(8,128)(2,1)S(1)} %pad_maximum_fusion.1), channel_id=1, source_target_pairs={{0,18},{1,19},{2,16},{3,17},{4,22},{5,23},{6,20},{7,21},{8,26},{9,... | collective-permute-start | bytes 1277960 | tf_op jit(solution)/shard_map/ppermute | solution.py:61
  15.6 9.4 %collective-permute-start.1 = (bf16[160,640]{1,0:T(8,128)(2,1)S(1)}, bf16[160,640]{1,0:T(8,128)(2,1)S(1)}, u32[]{:S(2)}, u32[]{:S(2)}) collective-permute-start(bf16[160,640]{1,0:T(8,128)(2,1)S(1)} %pad_maximum_fusion.2), channel_id=1, source_target_pairs={{0,224},{1,225},{2,226},{3,227},{4,228},{5,229},{6,230},{7,231},{8... | collective-permute-start | bytes 614408 | tf_op jit(solution)/shard_map/ppermute | solution.py:61
  21.5 7.2 %collective-permute-start.2 = (bf16[160,640]{1,0:T(8,128)(2,1)S(1)}, bf16[160,640]{1,0:T(8,128)(2,1)S(1)}, u32[]{:S(2)}, u32[]{:S(2)}) collective-permute-start(bf16[160,640]{1,0:T(8,128)(2,1)S(1)} %pad_maximum_fusion.2), channel_id=1, source_target_pairs={{0,32},{1,33},{2,34},{3,35},{4,36},{5,37},{6,38},{7,39},{8,40},{9,... | collective-permute-start | bytes 614408 | tf_op jit(solution)/shard_map/ppermute | solution.py:61
  25.0 7.0 %collective-permute-start.3 = (bf16[160,640]{1,0:T(8,128)(2,1)S(1)}, bf16[160,640]{1,0:T(8,128)(2,1)S(1)}, u32[]{:S(2)}, u32[]{:S(2)}) collective-permute-start(bf16[160,640]{1,0:T(8,128)(2,1)S(1)} %collective-permute-done.1), channel_id=1, source_target_pairs={{0,224},{1,225},{2,226},{3,227},{4,228},{5,229},{6,230},{7,231},{8... | collective-permute-start | bytes 614408 | tf_op jit(solution)/shard_map/ppermute | solution.py:61
  28.7 7.0 %collective-permute-start.4 = (bf16[160,640]{1,0:T(8,128)(2,1)S(1)}, bf16[160,640]{1,0:T(8,128)(2,1)S(1)}, u32[]{:S(2)}, u32[]{:S(2)}) collective-permute-start(bf16[160,640]{1,0:T(8,128)(2,1)S(1)} %collective-permute-done.2), channel_id=1, source_target_pairs={{0,32},{1,33},{2,34},{3,35},{4,36},{5,37},{6,38},{7,39},{8,40},{9,... | collective-permute-start | bytes 614408 | tf_op jit(solution)/shard_map/ppermute | solution.py:61
  32.0 11.3 %collective-permute-start.5 = (bf16[160,640]{1,0:T(8,128)(2,1)S(1)}, bf16[160,640]{1,0:T(8,128)(2,1)S(1)}, u32[]{:S(2)}, u32[]{:S(2)}) collective-permute-start(bf16[160,640]{1,0:T(8,128)(2,1)S(1)} %collective-permute-done.3), channel_id=1, source_target_pairs={{0,224},{1,225},{2,226},{3,227},{4,228},{5,229},{6,230},{7,231},{8... | collective-permute-start | bytes 614408 | tf_op jit(solution)/shard_map/ppermute | solution.py:61
  35.7 7.5 %collective-permute-start.6 = (bf16[160,640]{1,0:T(8,128)(2,1)S(1)}, bf16[160,640]{1,0:T(8,128)(2,1)S(1)}, u32[]{:S(2)}, u32[]{:S(2)}) collective-permute-start(bf16[160,640]{1,0:T(8,128)(2,1)S(1)} %collective-permute-done.4), channel_id=1, source_target_pairs={{0,32},{1,33},{2,34},{3,35},{4,36},{5,37},{6,38},{7,39},{8,40},{9,... | collective-permute-start | bytes 614408 | tf_op jit(solution)/shard_map/ppermute | solution.py:61
  43.2 5.9 %collective-permute-start.7 = (bf16[80,640]{1,0:T(8,128)(2,1)S(1)}, bf16[80,640]{1,0:T(8,128)(2,1)S(1)}, u32[]{:S(2)}, u32[]{:S(2)}) collective-permute-start(bf16[80,640]{1,0:T(8,128)(2,1)S(1)} %slice.98), channel_id=1, source_target_pairs={{0,32},{1,33},{2,34},{3,35},{4,36},{5,37},{6,38},{7,39},{8,40},{9,... | collective-permute-start | bytes 307208 | tf_op jit(solution)/shard_map/ppermute | solution.py:61
  49.2 6.6 %collective-permute-start.9 = (bf16[1280,640]{1,0:T(8,128)(2,1)S(1)}, bf16[1280,640]{1,0:T(8,128)(2,1)S(1)}, u32[]{:S(2)}, u32[]{:S(2)}) collective-permute-start(bf16[1280,640]{1,0:T(8,128)(2,1)S(1)} %constant_dynamic-update-slice_fusion.ka_ref), channel_id=1, source_target_pairs={{0,1},{1,0},{2,3},{3,2},{4,5},{5,4},{6,7},{7,6},{8,9},{9,8},{10,11... | collective-permute-start | bytes 4915208 | tf_op jit(solution)/shard_map/ppermute | solution.py:61
  79.5 11.0 %collective-permute-start.10 = (bf16[128,1152]{1,0:T(8,128)(2,1)S(1)}, bf16[128,1152]{1,0:T(8,128)(2,1)S(1)}, u32[]{:S(2)}, u32[]{:S(2)}) collective-permute-start(bf16[128,1152]{1,0:T(8,128)(2,1)S(1)} %concatenate.48), channel_id=1, source_target_pairs={{0,16},{1,17},{2,18},{3,19},{4,20},{5,21},{6,22},{7,23},{8,24},{9,... | collective-permute-start | bytes 884744 | tf_op jit(solution)/shard_map/ppermute | solution.py:61
  91.3 8.8 %collective-permute-start.11 = (bf16[128,1024]{1,0:T(8,128)(2,1)S(1)}, bf16[128,1024]{1,0:T(8,128)(2,1)S(1)}, u32[]{:S(2)}, u32[]{:S(2)}) collective-permute-start(bf16[128,1024]{1,0:T(8,128)(2,1)S(1)} %get-tuple-element.12), channel_id=1, source_target_pairs={{0,224},{1,225},{2,226},{3,227},{4,228},{5,229},{6,230},{7,231},{8... | collective-permute-start | bytes 786440 | tf_op jit(solution)/shard_map/ppermute | solution.py:61
  94.7 9.1 %collective-permute-start.12 = (bf16[128,1024]{1,0:T(8,128)(2,1)S(1)}, bf16[128,1024]{1,0:T(8,128)(2,1)S(1)}, u32[]{:S(2)}, u32[]{:S(2)}) collective-permute-start(bf16[128,1024]{1,0:T(8,128)(2,1)S(1)} %get-tuple-element.12), channel_id=1, source_target_pairs={{0,32},{1,33},{2,34},{3,35},{4,36},{5,37},{6,38},{7,39},{8,40},{9,... | collective-permute-start | bytes 786440 | tf_op jit(solution)/shard_map/ppermute | solution.py:61
  100.1 8.2 %collective-permute-start.13 = (bf16[128,1024]{1,0:T(8,128)(2,1)S(1)}, bf16[128,1024]{1,0:T(8,128)(2,1)S(1)}, u32[]{:S(2)}, u32[]{:S(2)}) collective-permute-start(bf16[128,1024]{1,0:T(8,128)(2,1)S(1)} %collective-permute-done.11), channel_id=1, source_target_pairs={{0,224},{1,225},{2,226},{3,227},{4,228},{5,229},{6,230},{7,231},{8... | collective-permute-start | bytes 786440 | tf_op jit(solution)/shard_map/ppermute | solution.py:61
  103.8 8.2 %collective-permute-start.14 = (bf16[128,1024]{1,0:T(8,128)(2,1)S(1)}, bf16[128,1024]{1,0:T(8,128)(2,1)S(1)}, u32[]{:S(2)}, u32[]{:S(2)}) collective-permute-start(bf16[128,1024]{1,0:T(8,128)(2,1)S(1)} %collective-permute-done.12), channel_id=1, source_target_pairs={{0,32},{1,33},{2,34},{3,35},{4,36},{5,37},{6,38},{7,39},{8,40},{9,... | collective-permute-start | bytes 786440 | tf_op jit(solution)/shard_map/ppermute | solution.py:61
  103.8 22.6 %collective-permute-start.19 = (bf16[1024,448]{0,1:T(8,128)(2,1)}, bf16[1024,448]{0,1:T(8,128)(2,1)}, u32[]{:S(2)}, u32[]{:S(2)}) collective-permute-start(bf16[1024,448]{0,1:T(8,128)(2,1)} %param.17), channel_id=1, source_target_pairs={{0,16},{1,17},{2,18},{3,19},{4,20},{5,21},{6,22},{7,23},{8,24},{9,... | collective-permute-start | bytes 2752520 | tf_op jit(solution)/shard_map/ppermute | solution.py:61
  108.4 11.4 %collective-permute-start.15 = (bf16[128,1024]{1,0:T(8,128)(2,1)S(1)}, bf16[128,1024]{1,0:T(8,128)(2,1)S(1)}, u32[]{:S(2)}, u32[]{:S(2)}) collective-permute-start(bf16[128,1024]{1,0:T(8,128)(2,1)S(1)} %collective-permute-done.13), channel_id=1, source_target_pairs={{0,224},{1,225},{2,226},{3,227},{4,228},{5,229},{6,230},{7,231},{8... | collective-permute-start | bytes 786440 | tf_op jit(solution)/shard_map/ppermute | solution.py:61
  112.0 7.6 %collective-permute-start.16 = (bf16[128,1024]{1,0:T(8,128)(2,1)S(1)}, bf16[128,1024]{1,0:T(8,128)(2,1)S(1)}, u32[]{:S(2)}, u32[]{:S(2)}) collective-permute-start(bf16[128,1024]{1,0:T(8,128)(2,1)S(1)} %collective-permute-done.14), channel_id=1, source_target_pairs={{0,32},{1,33},{2,34},{3,35},{4,36},{5,37},{6,38},{7,39},{8,40},{9,... | collective-permute-start | bytes 786440 | tf_op jit(solution)/shard_map/ppermute | solution.py:61
  119.6 6.3 %collective-permute-start.17 = (bf16[64,1024]{1,0:T(8,128)(2,1)S(1)}, bf16[64,1024]{1,0:T(8,128)(2,1)S(1)}, u32[]{:S(2)}, u32[]{:S(2)}) collective-permute-start(bf16[64,1024]{1,0:T(8,128)(2,1)S(1)} %slice.111), channel_id=1, source_target_pairs={{0,32},{1,33},{2,34},{3,35},{4,36},{5,37},{6,38},{7,39},{8,40},{9,... | collective-permute-start | bytes 393224 | tf_op jit(solution)/shard_map/ppermute | solution.py:61
  119.8 6.2 %collective-permute-start.18 = (bf16[64,1024]{1,0:T(8,128)(2,1)S(1)}, bf16[64,1024]{1,0:T(8,128)(2,1)S(1)}, u32[]{:S(2)}, u32[]{:S(2)}) collective-permute-start(bf16[64,1024]{1,0:T(8,128)(2,1)S(1)} %slice.112), channel_id=1, source_target_pairs={{0,224},{1,225},{2,226},{3,227},{4,228},{5,229},{6,230},{7,231},{8... | collective-permute-start | bytes 393224 | tf_op jit(solution)/shard_map/ppermute | solution.py:61
  134.2 8.5 %collective-permute-start.21 = (bf16[256,448]{0,1:T(8,128)(2,1)S(1)}, bf16[256,448]{0,1:T(8,128)(2,1)S(1)}, u32[]{:S(2)}, u32[]{:S(2)}) collective-permute-start(bf16[256,448]{0,1:T(8,128)(2,1)S(1)} %get-tuple-element.17), channel_id=1, source_target_pairs={{0,4},{1,5},{2,6},{3,7},{4,8},{5,9},{6,10},{7,11},{8,12},{9,13},{1... | collective-permute-start | bytes 688136 | tf_op jit(solution)/shard_map/ppermute | solution.py:61
  135.8 7.8 %collective-permute-start.22 = (bf16[256,448]{0,1:T(8,128)(2,1)S(1)}, bf16[256,448]{0,1:T(8,128)(2,1)S(1)}, u32[]{:S(2)}, u32[]{:S(2)}) collective-permute-start(bf16[256,448]{0,1:T(8,128)(2,1)S(1)} %get-tuple-element.19), channel_id=1, source_target_pairs={{0,12},{1,13},{2,14},{3,15},{4,0},{5,1},{6,2},{7,3},{8,4},{9,5},{1... | collective-permute-start | bytes 688136 | tf_op jit(solution)/shard_map/ppermute | solution.py:61
  136.3 12.6 %collective-permute-start.23 = (bf16[256,448]{0,1:T(8,128)(2,1)S(1)}, bf16[256,448]{0,1:T(8,128)(2,1)S(1)}, u32[]{:S(2)}, u32[]{:S(2)}) collective-permute-start(bf16[256,448]{0,1:T(8,128)(2,1)S(1)} %get-tuple-element.18), channel_id=1, source_target_pairs={{0,8},{1,9},{2,10},{3,11},{4,12},{5,13},{6,14},{7,15},{8,0},{9,1},... | collective-permute-start | bytes 688136 | tf_op jit(solution)/shard_map/ppermute | solution.py:61
  149.0 12.5 %collective-permute-start.24 = (bf16[128,448]{0,1:T(8,128)(2,1)S(1)}, bf16[128,448]{0,1:T(8,128)(2,1)S(1)}, u32[]{:S(2)}, u32[]{:S(2)}) collective-permute-start(bf16[128,448]{0,1:T(8,128)(2,1)S(1)} %get-tuple-element.22), channel_id=1, source_target_pairs={{0,0},{1,1},{2,32},{3,33},{4,224},{5,225},{6,64},{7,65},{8,192},{9... | collective-permute-start | bytes 344072 | tf_op jit(solution)/shard_map/ppermute | solution.py:61
  150.9 18.1 %collective-permute-start.25 = (bf16[128,448]{0,1:T(8,128)(2,1)S(1)}, bf16[128,448]{0,1:T(8,128)(2,1)S(1)}, u32[]{:S(2)}, u32[]{:S(2)}) collective-permute-start(bf16[128,448]{0,1:T(8,128)(2,1)S(1)} %get-tuple-element.23), channel_id=1, source_target_pairs={{0,32},{1,33},{2,0},{3,1},{4,64},{5,65},{6,224},{7,225},{8,96},{9,... | collective-permute-start | bytes 344072 | tf_op jit(solution)/shard_map/ppermute | solution.py:61
  (10 other events, 60.1 us)
